TPU v7x, 512 devices: a whole 4x8x8 slice. The times are simulated.
512 devices in a mesh: wide: 32 (over y, x), narrow: 16 (over z, core).
Axes of the slice: x: 4, y: 8, z: 8, core: 2. Of those that a mesh axis runs over, the one named last changes fastest.
Arguments:
- hamiltonian: float32 [1024, 3, 128, 128], P(('wide', 'narrow')), may hold values from -3.3 to 3.3, as said below
- old_density: float32 [1024, 3, 128, 128], P(('wide', 'narrow')), may hold values from -2 to 2
- neighbours: int32 [1024, 3], P(('wide', 'narrow')), may hold values from 0 to 31, as said below
- live: int32 [1024], P(('wide', 'narrow')), may hold values from 0 to 1, as said below
- potential: float32 [1], replicated, may hold values from -1 to 1
Outputs:
- density: float32 [1024, 3, 128, 128], P(('wide', 'narrow'))
Inputs may be any that keep to these rules, and one draw needn't show every extreme that they name: Within each cluster of 32 consecutive blocks, entry 0 is the block's own index in the cluster and entries 1 and 2 are its neighbours on a cycle through all blocks of the cluster: block a is entry 1 of its entry-2 neighbour and entry 2 of its entry-1 neighbour. Along the cycle the 2 blocks of one device stand next to each other in some order; the devices of the narrow axis follow each other in an order drawn from the seed. For each index of the narrow axis, the devices at wide indices i and i + 16 own at most 2 live blocks together; in every draw some device owns 2 live blocks. `hamiltonian`: the block Hamiltonian is symmetric: tile 1 of block c is the transpose of tile 2 of prev(c), and tile 0 is symmetric.
All inputs are finite; a program needn't handle non-finite values. Where the computation divides by a largest or mean magnitude, that divisor is 1e-20 or more.
Results may differ from a plain program's by a relative error of at most 0.0001.
Values sent between devices are 32-bit elements; how exact they have to be, the bound alone decides.
A program may use at most 64 MiB of HBM per device.

v0:
```python
import jax
import jax.numpy as jnp
from jax import lax
from jax.sharding import PartitionSpec as P

ITERS = 4
epsilon = 1e-06


def in_one_piece(arrays, axis, dim, along):
    widths = [a.shape[along] for a in arrays]
    both = jnp.concatenate(arrays, axis=along)
    out = lax.all_gather(both, axis, axis=dim, tiled=True)
    return tuple(jnp.split(out, [sum(widths[:k]) for k in range(1, len(widths))], axis=along))


def product(left, right):
    return jnp.matmul(left, right, precision=lax.Precision.HIGHEST)


def transpose_tiles(tiles):
    return jnp.swapaxes(tiles, -1, -2)


def assemble(row_tiles, prev_onsite, next_onsite, level):
    zero_tile = jnp.zeros_like(prev_onsite)
    upper_rows = jnp.concatenate(
        [row_tiles[..., 0, :, :], row_tiles[..., 1, :, :], row_tiles[..., 2, :, :]], axis=-1
    )
    middle_rows = jnp.concatenate(
        [transpose_tiles(row_tiles[..., 1, :, :]), prev_onsite, zero_tile], axis=-1
    )
    lower_rows = jnp.concatenate(
        [transpose_tiles(row_tiles[..., 2, :, :]), zero_tile, next_onsite], axis=-1
    )
    matrix = jnp.concatenate([upper_rows, middle_rows, lower_rows], axis=-2)
    order = matrix.shape[-1]
    return matrix - level * jnp.eye(order, dtype=jnp.float32)


def sign_columns(matrix, width, depth):
    order = matrix.shape[-1]
    identity = jnp.eye(order, dtype=jnp.float32)
    bound = jnp.max(jnp.sum(jnp.abs(matrix), axis=-1), axis=-1) + epsilon
    current = matrix / bound[..., None, None]
    for sweep in range(depth - 1):
        square = product(current, current)
        current = 0.5 * product(current, 3.0 * identity - square)
    square = product(current, current)
    final_cols = 0.5 * product(current, 3.0 * identity[:, :width] - square[..., :, :width])
    columns = 0.5 * (identity[:, :width] - final_cols)
    return columns.reshape(columns.shape[:-2] + (order // width, width, width))


def shards(hamiltonian, old_density, neighbours, live, potential):
    width = hamiltonian.shape[-1]
    level = potential[0]
    cluster_onsite = lax.all_gather(hamiltonian[:, 0], "narrow", axis=0, tiled=True)
    prev_onsite = jnp.take(cluster_onsite, neighbours[:, 1], axis=0)
    next_onsite = jnp.take(cluster_onsite, neighbours[:, 2], axis=0)
    matrices = assemble(hamiltonian, prev_onsite, next_onsite, level)
    new_cols = sign_columns(matrices, width, ITERS)
    fresh_cols = jnp.where(live[:, None, None, None] == 1, new_cols, old_density)
    prev_side, next_side = in_one_piece((fresh_cols[:, 1], fresh_cols[:, 2]), "narrow", 0, 1)
    from_prev = jnp.take(next_side, neighbours[:, 1], axis=0)
    from_next = jnp.take(prev_side, neighbours[:, 2], axis=0)
    return jnp.stack(
        [
            0.5 * (fresh_cols[:, 0] + transpose_tiles(fresh_cols[:, 0])),
            0.5 * (fresh_cols[:, 1] + transpose_tiles(from_prev)),
            0.5 * (fresh_cols[:, 2] + transpose_tiles(from_next)),
        ],
        axis=1,
    )


def solution(mesh):
    placed = (
        P(("wide", "narrow"), None, None, None),
        P(("wide", "narrow"), None, None, None),
        P(("wide", "narrow"), None),
        P(("wide", "narrow")),
        P(),
    )
    return jax.shard_map(
        shards,
        mesh=mesh,
        in_specs=placed,
        out_specs=P(("wide", "narrow"), None, None, None),
        check_vma=False,
    )
```

profile of v0, /device:TPU:1, one launch (start us, length us, event | category | flops | bytes accessed | tf_op | source)
XLA Modules:
  0.0 140.7 jit_solution(15930580519983071181)
XLA Ops:
  6.5 1.8 %slice_bitcast_fusion.5 = (f32[2,128,128]{2,1,0:T(8,128)S(1)}, f32[2,128,128]{2,1,0:T(8,128)S(1)}, f32[2,128,128]{2,1,0:T(8,128)S(1)}, f32[2,1,128,128]{3,2,1,0:...) fusion(f32[2,3,128,128]{3,2,1,0:T(8,128)} %param.7), kind=kLoop, calls=%fused_computation.51 | loop fusion | bytes 1179648 | tf_op jit(solution)/shard_map/squeeze | solution.py:28
  9.0 0.1 copy.68
  9.1 0.1 copy.69
  9.2 0.2 slice_reduce_fusion.1
  9.7 48.9 %all-gather.6.cloned.1.call-done = f32[32,1,128,128]{3,2,1,0:T(8,128)} async-done(((f32[2,1,128,128]{3,2,1,0:T(8,128)}), f32[32,1,128,128]{3,2,1,0:T(8,128)}) %all-gather.6.cloned.1.call-update) | async-done | bytes 2097168 | tf_op jit(solution)/shard_map/all_gather | solution.py:58
  58.6 2.1 %gather_fusion.1 = f32[2,128,128]{2,1,0:T(8,128)S(1)} fusion(f32[32,128,128]{2,1,0:T(8,128)} %bitcast.68, s32[1024]{0:T(1024)S(1)} %pad_clamp_fusion), kind=kCustom, calls=%fused_computation.1.clone | custom fusion | bytes 262152 | tf_op jit(solution)/shard_map/jit(_take)/gather | solution.py:60
  60.8 2.1 %gather_fusion = f32[2,128,128]{2,1,0:T(8,128)S(1)} fusion(f32[32,128,128]{2,1,0:T(8,128)} %bitcast.69, s32[1024]{0:T(1024)S(1)} %pad_clamp_fusion.1), kind=kCustom, calls=%fused_computation.clone | custom fusion | bytes 262152 | tf_op jit(solution)/shard_map/jit(_take)/gather | solution.py:59
  62.9 0.1 broadcast_select_fusion.1
  63.0 0.1 broadcast_select_fusion
  63.1 0.2 abs_reduce_fusion
  63.3 0.1 reduce_max.9
  63.5 2.6 %convolution_subtract_fusion.2 = f32[2,384,384]{2,1,0:T(8,128)S(1)} fusion(f32[384,384]{1,0:T(8,128)S(1)} %fusion.3, f32[2]{0:T(128)S(1)} %broadcast_add_fusion, f32[2,128,128]{2,1,0:T(8,128)S(1)} %broadcast_select_fusion, f32[2,128,128]{2,1,0:T(8,128)S(1)} %broadcast_in_dim.17, f32[2,128,128]{2,1,0:T(8,128)S(1)} %bitcast.66, ...), kind=kOutput, calls=%fused_computation.9 | convolution fusion | flops 1362198528 | bytes 3407880 | tf_op jit(solution)/shard_map/dot_general | solution.py:18
  66.1 2.5 %convolution_multiply_fusion.2 = f32[2,384,384]{2,1,0:T(8,128)S(1)} fusion(f32[2,384,384]{2,1,0:T(8,128)S(1)} %convolution_subtract_fusion.2, f32[2]{0:T(128)S(1)} %broadcast_add_fusion, f32[2,128,128]{2,1,0:T(8,128)S(1)} %broadcast_select_fusion, f32[2,128,128]{2,1,0:T(8,128)S(1)} %broadcast_in_dim.17, f32[2,128,128]{2,1,0:T(8,128)S(1)} %bitcast.67, ...), kind=kOutput, calls=%fused_computation.8 | convolution fusion | flops 1362198528 | bytes 3997704 | tf_op jit(solution)/shard_map/dot_general | solution.py:18
  68.6 2.5 %convolution_subtract_fusion.1 = f32[2,384,384]{2,1,0:T(8,128)S(1)} fusion(f32[2,384,384]{2,1,0:T(8,128)S(1)} %convolution_multiply_fusion.2, f32[384,384]{1,0:T(8,128)S(1)} %fusion.3), kind=kOutput, calls=%fused_computation.7 | convolution fusion | flops 1359249408 | bytes 2949120 | tf_op jit(solution)/shard_map/dot_general | solution.py:18
  71.1 2.4 %convolution_multiply_fusion.1 = f32[2,384,384]{2,1,0:T(8,128)S(1)} fusion(f32[2,384,384]{2,1,0:T(8,128)S(1)} %convolution_multiply_fusion.2, f32[2,384,384]{2,1,0:T(8,128)S(1)} %convolution_subtract_fusion.1), kind=kOutput, calls=%fused_computation.6 | convolution fusion | flops 1359249408 | bytes 3538944 | tf_op jit(solution)/shard_map/dot_general | solution.py:18
  73.5 2.7 %convolution_subtract_fusion = f32[2,384,384]{2,1,0:T(8,128)S(1)} fusion(f32[2,384,384]{2,1,0:T(8,128)S(1)} %convolution_multiply_fusion.1, f32[384,384]{1,0:T(8,128)S(1)} %fusion.3), kind=kOutput, calls=%fused_computation.5 | convolution fusion | flops 1359249408 | bytes 2949120 | tf_op jit(solution)/shard_map/dot_general | solution.py:18
  76.2 2.4 %convolution_multiply_fusion = f32[2,384,384]{2,1,0:T(8,128)S(1)} fusion(f32[2,384,384]{2,1,0:T(8,128)S(1)} %convolution_multiply_fusion.1, f32[2,384,384]{2,1,0:T(8,128)S(1)} %convolution_subtract_fusion), kind=kOutput, calls=%fused_computation.4 | convolution fusion | flops 1359249408 | bytes 3538944 | tf_op jit(solution)/shard_map/dot_general | solution.py:18
  78.7 1.2 convolution_subtract_fusion.3
  79.9 1.2 fusion.1
  81.1 0.1 copy_select_fusion
  81.2 0.7 pad_maximum_fusion.1
  81.9 0.1 copy.63
  82.0 0.1 copy.62
  82.2 43.7 %all-gather.4.cloned.1.call-done = f32[32,256,128]{2,1,0:T(8,128)} async-done(((f32[2,256,128]{2,1,0:T(8,128)}), f32[32,256,128]{2,1,0:T(8,128)}) %all-gather.4.cloned.1.call-update) | async-done | bytes 4194320 | tf_op jit(solution)/shard_map/all_gather | solution.py:13
  125.9 3.9 %fusion.9 = (f32[32,128,128]{2,1,0:T(8,128)}, f32[32,128,128]{2,1,0:T(8,128)S(1)}) fusion(f32[32,256,128]{2,1,0:T(8,128)} %all-gather.4.cloned.1.call-done), kind=kLoop, calls=%fused_computation.52 | loop fusion | bytes 8388608 | tf_op jit(solution)/shard_map/split | solution.py:14
  129.8 2.1 %gather_fusion.2 = f32[2,128,128]{2,1,0:T(8,128)S(1)} fusion(f32[32,128,128]{2,1,0:T(8,128)} %get-tuple-element.8, s32[1024]{0:T(1024)S(1)} %pad_clamp_fusion.1), kind=kCustom, calls=%fused_computation.2.clone | custom fusion | bytes 262152 | tf_op jit(solution)/shard_map/jit(_take)/gather | solution.py:65
  131.9 0.6 gather_fusion.3
  132.5 0.1 copy.64
  132.6 0.1 bitcast_add_fusion.1
  132.7 0.1 copy.65
  132.8 0.1 fusion.8
  132.9 0.9 copy.66
  (26 shorter events, 0.4 us)
Async XLA Ops:
  6.5 2.7 %copy-start.1 = (s32[2,3]{1,0:T(2,128)S(1)}, s32[2,3]{1,0:T(2,128)}, u32[]{:S(2)}) copy-start(s32[2,3]{1,0:T(2,128)} %param.9) | copy-start | bytes 76
  6.5 52.1 %all-gather.6.cloned.1.call-start = ((), (), s32[]{:S(2)}) async-start(), calls=%async_computation.1 | async-start | bytes 2228224 | tf_op jit(solution)/shard_map/all_gather | solution.py:58
  8.3 1.3 copy-start.2
  8.3 117.5 %all-gather.4.cloned.1.call-start = ((), (), s32[]{:S(2)}) async-start(), calls=%async_computation | async-start | bytes 4456448 | tf_op jit(solution)/shard_map/all_gather | solution.py:13
  79.8 1.2 copy-start
Sparse Core Ops, SparseCore 0:
  9.5 49.0 all-gather.5
  82.1 43.7 all-gather.3
where the time goes:
time: 141 us
  waiting for transfers between devices  92.6 us (66%)
  matrix products  17.5 us (12%)
  local copies, waits for them, and re-layouts  14.4 us (10%)
  between operations  14.3 us (10%)
  other arithmetic  1.79 us (1%)
    all_gather x1, waiting for transfers between devices, shards(): lax.all_gather(hamiltonian[:, 0], 'narrow', axis=0, tiled=True)  48.9 us
    all_gather x1, waiting for transfers between devices, in_one_piece(): out = lax.all_gather(both, axis, axis=dim, tiled=True)  43.7 us
    dot_general x8, matrix products, product(): return jnp.matmul(left, right, precision=lax.Precision.HIGHEST)  17.5 us
    split x1, local copies, waits for them, and re-layouts, in_one_piece(): jnp.split(out, [sum(widths[:k]) for k in range(1, len(widths))], axis=along)  3.92 us
  transfers between devices with their start and end apart: 2, of which 2 were waited for; matrix products, arithmetic and copies ran while one was open for 1% of the time, Pallas kernels for 0%

commit v1 on v0

--- a/solution.py
+++ b/solution.py
@@ -55,7 +55,10 @@
 def shards(hamiltonian, old_density, neighbours, live, potential):
     width = hamiltonian.shape[-1]
     level = potential[0]
-    cluster_onsite = lax.all_gather(hamiltonian[:, 0], "narrow", axis=0, tiled=True)
+    cluster_onsite = jnp.concatenate(
+        lax.all_to_all(jnp.stack([hamiltonian[:, 0]] * lax.axis_size("narrow")), "narrow", 0, 0),
+        axis=0,
+    )
     prev_onsite = jnp.take(cluster_onsite, neighbours[:, 1], axis=0)
     next_onsite = jnp.take(cluster_onsite, neighbours[:, 2], axis=0)
     matrices = assemble(hamiltonian, prev_onsite, next_onsite, level)

time: 141 us -> 154 us (1.092)
  starting transfers between devices: 0.04 us -> 12 us
  other arithmetic: 1.79 us -> 5.66 us
  waiting for transfers between devices: 92.6 us -> 89.1 us
    all_gather x1 -> x0, waiting for transfers between devices: 48.9 us -> none  [shards(): lax.all_gather(hamiltonian[:, 0], 'narrow', axis=0, tiled=True)]
    all_to_all x0 -> x1, waiting for transfers between devices: none -> 44.5 us  [shards(): lax.all_to_all(jnp.stack([hamiltonian[:, 0]] * lax.axis_size('narrow')),...]
    all_to_all x0 -> x1, starting transfers between devices: none -> 12 us  [shards(): lax.all_to_all(jnp.stack([hamiltonian[:, 0]] * lax.axis_size('narrow')),...]
    gather x1, local copies, waits for them, and re-layouts: 2.14 us -> 0.56 us  [shards(): next_onsite = jnp.take(cluster_onsite, neighbours[:, 2], axis=0)]
    another operation x0 -> x1, local copies, waits for them, and re-layouts: none -> 1.58 us  [shards(): jnp.stack([hamiltonian[:, 0]] * lax.axis_size('narrow'))]
  transfers between devices with their start and end apart: 2 -> 2, of which waited for: 2 -> 2; matrix products, arithmetic and copies ran while one was open for 1% -> 3% of each run, Pallas kernels for 0% -> 0%
where the time goes in v1:
time: 154 us; the launch traced here: 153 us
  waiting for transfers between devices  89.1 us (58%)
  matrix products  17.4 us (11%)
  local copies, waits for them, and re-layouts  14.8 us (10%)
  between operations  14.4 us (9%)
  starting transfers between devices  12 us (8%)
  other arithmetic  5.66 us (4%)
    all_gather x1, waiting for transfers between devices, in_one_piece(): out = lax.all_gather(both, axis, axis=dim, tiled=True)  44.7 us
    all_to_all x1, waiting for transfers between devices, shards(): lax.all_to_all(jnp.stack([hamiltonian[:, 0]] * lax.axis_size('narrow')),...  44.5 us
    dot_general x8, matrix products, product(): return jnp.matmul(left, right, precision=lax.Precision.HIGHEST)  17.4 us
    all_to_all x1, starting transfers between devices, shards(): lax.all_to_all(jnp.stack([hamiltonian[:, 0]] * lax.axis_size('narrow')),...  12 us
    split x1, local copies, waits for them, and re-layouts, in_one_piece(): jnp.split(out, [sum(widths[:k]) for k in range(1, len(widths))], axis=along)  3.93 us
  transfers between devices with their start and end apart: 2, of which 2 were waited for; matrix products, arithmetic and copies ran while one was open for 3% of the time, Pallas kernels for 0%

profile of v1, /device:TPU:1, one launch (start us, length us, event | category | flops | bytes accessed | tf_op | source)
XLA Modules:
  0.0 153.4 jit_solution(16390120345698410963)
XLA Ops:
  6.5 1.8 %slice_bitcast_fusion.5 = (f32[2,128,128]{2,1,0:T(8,128)}, f32[2,128,128]{2,1,0:T(8,128)}, f32[2,1,128,128]{3,2,1,0:T(8,128)S(1)}, f32[2,128,128]{2,1,0:T(8,128)S(1)}, f32[2,1,128,128]{3,2,1,0:T(8,128)S(1)}) fusion(f32[2,3,128,128]{3,2,1,0:T(8,128)} %param.7), kind=kLoop, calls=%fused_computation.51 | loop fusion | bytes 1048576 | tf_op jit(solution)/shard_map/squeeze | solution.py:28
  8.3 1.6 %stack.15 = f32[16,2,128,128]{3,2,1,0:T(8,128)} broadcast(f32[2,128,128]{2,1,0:T(8,128)S(1)} %get-tuple-element.16), dimensions={1,2,3} | broadcast | bytes 2228224 | tf_op jit(solution)/shard_map/stack | solution.py:59
  9.9 12.0 %all-to-all-start = ((f32[16,2,128,128]{3,2,1,0:T(8,128)}), f32[16,2,128,128]{3,2,1,0:T(8,128)S(1)}, u32[]{:S(2)}, u32[]{:S(2)}) async-start(f32[16,2,128,128]{3,2,1,0:T(8,128)} %stack.15), calls=%async_computation | async-start | bytes 4194304 | tf_op jit(solution)/shard_map/all_to_all | solution.py:59
  22.6 0.7 copy.62
  23.3 0.7 copy.63
  24.1 0.2 slice_reduce_fusion.1
  24.5 0.5 broadcast_compare_fusion
  25.0 0.7 slice_select_fusion
  25.7 0.7 slice_convert_fusion
  26.3 44.5 %all-to-all-done = f32[16,2,128,128]{3,2,1,0:T(8,128)S(1)} async-done(((f32[16,2,128,128]{3,2,1,0:T(8,128)}), f32[16,2,128,128]{3,2,1,0:T(8,128)S(1)}, u32[]{:S(2)}, u32[]{:S(2)}) %all-to-all-start) | async-done | bytes 2097184 | tf_op jit(solution)/shard_map/all_to_all | solution.py:59
  70.8 0.6 gather_fusion.1
  71.4 1.2 gather_fusion
  72.6 1.0 broadcast_select_fusion.1
  73.7 1.3 abs_reduce_fusion
  75.1 0.1 reduce_max.9
  75.2 2.6 %convolution_subtract_fusion.2 = f32[2,384,384]{2,1,0:T(8,128)S(1)} fusion(f32[384,384]{1,0:T(8,128)S(1)} %fusion.3, f32[2]{0:T(128)S(1)} %broadcast_add_fusion, f32[2,128,128]{2,1,0:T(8,128)S(1)} %broadcast_select_fusion, f32[2,128,128]{2,1,0:T(8,128)S(1)} %broadcast_in_dim.17, f32[2,128,128]{2,1,0:T(8,128)S(1)} %bitcast.64, ...), kind=kOutput, calls=%fused_computation.9 | convolution fusion | flops 1362198528 | bytes 3407880 | tf_op jit(solution)/shard_map/dot_general | solution.py:18
  77.9 2.4 %convolution_multiply_fusion.2 = f32[2,384,384]{2,1,0:T(8,128)S(1)} fusion(f32[2,384,384]{2,1,0:T(8,128)S(1)} %convolution_subtract_fusion.2, f32[2]{0:T(128)S(1)} %broadcast_add_fusion, f32[2,128,128]{2,1,0:T(8,128)S(1)} %broadcast_select_fusion, f32[2,128,128]{2,1,0:T(8,128)S(1)} %broadcast_in_dim.17, f32[2,128,128]{2,1,0:T(8,128)S(1)} %bitcast.65, ...), kind=kOutput, calls=%fused_computation.8 | convolution fusion | flops 1362198528 | bytes 3997704 | tf_op jit(solution)/shard_map/dot_general | solution.py:18
  80.3 2.5 %convolution_subtract_fusion.1 = f32[2,384,384]{2,1,0:T(8,128)S(1)} fusion(f32[2,384,384]{2,1,0:T(8,128)S(1)} %convolution_multiply_fusion.2, f32[384,384]{1,0:T(8,128)S(1)} %fusion.3), kind=kOutput, calls=%fused_computation.7 | convolution fusion | flops 1359249408 | bytes 2949120 | tf_op jit(solution)/shard_map/dot_general | solution.py:18
  82.8 2.4 %convolution_multiply_fusion.1 = f32[2,384,384]{2,1,0:T(8,128)S(1)} fusion(f32[2,384,384]{2,1,0:T(8,128)S(1)} %convolution_multiply_fusion.2, f32[2,384,384]{2,1,0:T(8,128)S(1)} %convolution_subtract_fusion.1), kind=kOutput, calls=%fused_computation.6 | convolution fusion | flops 1359249408 | bytes 3538944 | tf_op jit(solution)/shard_map/dot_general | solution.py:18
  85.2 2.7 %convolution_subtract_fusion = f32[2,384,384]{2,1,0:T(8,128)S(1)} fusion(f32[2,384,384]{2,1,0:T(8,128)S(1)} %convolution_multiply_fusion.1, f32[384,384]{1,0:T(8,128)S(1)} %fusion.3), kind=kOutput, calls=%fused_computation.5 | convolution fusion | flops 1359249408 | bytes 2949120 | tf_op jit(solution)/shard_map/dot_general | solution.py:18
  87.9 2.4 %convolution_multiply_fusion = f32[2,384,384]{2,1,0:T(8,128)S(1)} fusion(f32[2,384,384]{2,1,0:T(8,128)S(1)} %convolution_multiply_fusion.1, f32[2,384,384]{2,1,0:T(8,128)S(1)} %convolution_subtract_fusion), kind=kOutput, calls=%fused_computation.4 | convolution fusion | flops 1359249408 | bytes 3538944 | tf_op jit(solution)/shard_map/dot_general | solution.py:18
  90.4 1.2 convolution_subtract_fusion.3
  91.6 1.2 fusion.1
  92.8 0.1 copy_select_fusion
  93.0 0.7 pad_maximum_fusion.1
  93.7 0.1 copy.58
  93.8 0.1 copy.57
  93.9 44.7 %all-gather.2.cloned.1.call-done = f32[32,256,128]{2,1,0:T(8,128)} async-done(((f32[2,256,128]{2,1,0:T(8,128)}), f32[32,256,128]{2,1,0:T(8,128)}) %all-gather.2.cloned.1.call-update) | async-done | bytes 4194320 | tf_op jit(solution)/shard_map/all_gather | solution.py:13
  138.6 3.9 %fusion.9 = (f32[32,128,128]{2,1,0:T(8,128)}, f32[32,128,128]{2,1,0:T(8,128)S(1)}) fusion(f32[32,256,128]{2,1,0:T(8,128)} %all-gather.2.cloned.1.call-done), kind=kLoop, calls=%fused_computation.52 | loop fusion | bytes 8388608 | tf_op jit(solution)/shard_map/split | solution.py:14
  142.5 2.1 %gather_fusion.2 = f32[2,128,128]{2,1,0:T(8,128)S(1)} fusion(f32[32,128,128]{2,1,0:T(8,128)} %get-tuple-element.8, s32[1024]{0:T(1024)S(1)} %pad_clamp_fusion.1), kind=kCustom, calls=%fused_computation.2.clone | custom fusion | bytes 262152 | tf_op jit(solution)/shard_map/jit(_take)/gather | solution.py:68
  144.7 0.6 gather_fusion.3
  145.7 0.9 copy.61
  (40 shorter events, 0.8 us)
Async XLA Ops:
  9.9 14.2 %copy-start.7 = (s32[2,3]{1,0:T(2,128)S(1)}, s32[2,3]{1,0:T(2,128)}, u32[]{:S(2)}) copy-start(s32[2,3]{1,0:T(2,128)} %param.9) | copy-start | bytes 76
  9.9 60.9 %all-to-all-start = ((f32[16,2,128,128]{3,2,1,0:T(8,128)}), f32[16,2,128,128]{3,2,1,0:T(8,128)S(1)}, u32[]{:S(2)}, u32[]{:S(2)}) async-start(f32[16,2,128,128]{3,2,1,0:T(8,128)} %stack.15), calls=%async_computation | async-start | bytes 4194304 | tf_op jit(solution)/shard_map/all_to_all | solution.py:59
  21.9 2.6 %copy-start.9 = (s32[2]{0:T(128)S(1)}, s32[2]{0:T(128)}, u32[]{:S(2)}) copy-start(s32[2]{0:T(128)} %param.10) | copy-start | bytes 28
  21.9 116.7 %all-gather.2.cloned.1.call-start = ((), (), s32[]{:S(2)}) async-start(), calls=%async_computation.1 | async-start | bytes 4456448 | tf_op jit(solution)/shard_map/all_gather | solution.py:13
  72.6 2.6 %copy-start.2 = (f32[2,1,128,128]{2,3,0,1:T(8,128)S(1)}, f32[2,1,128,128]{2,3,0,1:T(8,128)}, u32[]{:S(2)}) copy-start(f32[2,1,128,128]{2,3,0,1:T(8,128)} %copy.62) | copy-start | bytes 393220
  72.6 2.6 %copy-start.3 = (f32[2,1,128,128]{2,3,0,1:T(8,128)S(1)}, f32[2,1,128,128]{2,3,0,1:T(8,128)}, u32[]{:S(2)}) copy-start(f32[2,1,128,128]{2,3,0,1:T(8,128)} %copy.63) | copy-start | bytes 393220
  72.6 2.6 %copy-start.4 = (f32[2,128,128]{2,1,0:T(8,128)S(1)}, f32[2,128,128]{2,1,0:T(8,128)}, u32[]{:S(2)}) copy-start(f32[2,128,128]{2,1,0:T(8,128)} %get-tuple-element.13) | copy-start | bytes 393220
  72.6 2.6 %copy-start.5 = (f32[2,128,128]{2,1,0:T(8,128)S(1)}, f32[2,128,128]{2,1,0:T(8,128)}, u32[]{:S(2)}) copy-start(f32[2,128,128]{2,1,0:T(8,128)} %get-tuple-element.14) | copy-start | bytes 393220
  87.9 2.5 %copy-start.1 = (f32[384,128]{1,0:T(8,128)S(1)}, f32[384,128]{1,0:T(8,128)}, u32[]{:S(2)}) copy-start(f32[384,128]{1,0:T(8,128)} %slice_select_fusion) | copy-start | bytes 589828
  90.4 1.2 copy-start
  91.6 1.2 copy-start.6
  91.6 1.2 copy-start.8
Sparse Core Ops, SparseCore 0:
  93.8 44.7 all-gather.1
